TPU v7x, 32 devices: a whole 2x2x4 slice. The times are simulated.
32 devices in a mesh: dp: 4 (over y, core), tensor: 2 (over x), expert: 4 (over z).
Axes of the slice: x: 2, y: 2, z: 4, core: 2. Of those that a mesh axis runs over, the one named last changes fastest.
Arguments:
- tokens: bfloat16 [512, 4096], P(('tensor', 'expert'), 'dp'), may hold values from -6 to 6
- routes: int32 [512, 8], P(('tensor', 'expert')), may hold values from 0 to 63, as said below
- gate_probs: float32 [512, 8], P(('tensor', 'expert')), may hold values from 0.05 to 0.5
- w_gate: bfloat16 [64, 4096, 1536], P(('tensor', 'expert'), 'dp'), may hold values from -0.09375 to 0.09375
- w_up: bfloat16 [64, 4096, 1536], P(('tensor', 'expert'), 'dp'), may hold values from -0.09375 to 0.09375
- w_down: bfloat16 [64, 1536, 4096], P(('tensor', 'expert'), None, 'dp'), may hold values from -0.15625 to 0.15625
Outputs:
- combined: bfloat16 [512, 4096], P(('tensor', 'expert'), 'dp')
Inputs may be any that keep to these rules, and one draw needn't show every extreme that they name: `routes`: each token names 8 different experts. In each aligned block of 64 rows no expert is named more than 16 times, and in every block some expert is named exactly 16 times.
All inputs are finite; a program needn't handle non-finite values.
Results may differ from a plain program's by a relative error of at most 0.019.
Values may be sent and summed in bfloat16 or wider, within the bound.
A program may use at most 192 MiB of HBM per device.

v0:
```python
import functools

import jax
import jax.numpy as jnp
from jax import lax
from jax.experimental import pallas as pl
from jax.experimental.pallas import tpu as pltpu
from jax.sharding import PartitionSpec as P

BF = jnp.bfloat16
F32 = jnp.float32
CORES = 2


def cut(total, tile):
    return [(at, min(tile, total - at)) for at in range(0, total, tile)]


def gather_kernel(n_x, n_z, tok_ref, info_ref, tok_out, info_out, zs, zr, xs, xr):
    x, z = lax.axis_index("tensor"), lax.axis_index("expert")
    pairs = ((tok_ref, tok_out), (info_ref, info_out))

    def along_z(k, i):
        src, dst = pairs[i]
        return pltpu.make_async_remote_copy(
            src, dst.at[x * n_z + z], zs.at[k - 1, i], zr.at[k - 1, i],
            device_id={"expert": lax.rem(z + k, n_z)})

    def along_x(k, j, i):
        src, dst = pairs[i]
        block = x * n_z + lax.rem(z - k + n_z, n_z)
        return pltpu.make_async_remote_copy(
            src if k == 0 else dst.at[block], dst.at[block], xs.at[k, j - 1, i], xr.at[k, j - 1, i],
            device_id={"tensor": lax.rem(x + j, n_x)})

    barrier = pltpu.get_barrier_semaphore()
    for k in range(1, n_z):
        pl.semaphore_signal(barrier, inc=1, device_id={"expert": lax.rem(z + k, n_z)})
    for j in range(1, n_x):
        pl.semaphore_signal(barrier, inc=1, device_id={"tensor": lax.rem(x + j, n_x)})
    pl.semaphore_wait(barrier, n_z + n_x - 2)

    offsets = sorted(range(1, n_z), key=lambda k: min(k, n_z - k))
    for i in (1, 0):
        for j in range(1, n_x):
            along_x(0, j, i).start()
        for k in offsets:
            along_z(k, i).start()
    for src, dst in pairs:
        dst[x * n_z + z] = src[...]
    for i in (1, 0):
        for k in offsets:
            along_z(k, i).wait_recv()
            for j in range(1, n_x):
                along_x(k, j, i).start()
    for i in (1, 0):
        for k in range(n_z):
            for j in range(1, n_x):
                along_x(k, j, i).wait()
        for k in offsets:
            along_z(k, i).wait_send()


def gather_all(n_x, n_z, tokens, info):
    inside = pl.BlockSpec(memory_space=pltpu.VMEM)
    dma = pltpu.SemaphoreType.DMA
    owners = n_x * n_z
    return pl.pallas_call(
        functools.partial(gather_kernel, n_x, n_z),
        out_shape=[jax.ShapeDtypeStruct((owners,) + a.shape, a.dtype) for a in (tokens, info)],
        in_specs=[inside] * 2,
        out_specs=[inside] * 2,
        scratch_shapes=[
            dma((n_z - 1, 2)), dma((n_z - 1, 2)), dma((n_z, n_x - 1, 2)), dma((n_z, n_x - 1, 2))],
        compiler_params=pltpu.CompilerParams(
            collective_id=3, has_side_effects=True, vmem_limit_bytes=32 * 1024 * 1024),
    )(tokens, info)


def experts_kernel(
    n_y, n_x, n_z, base, pool, unit, full_rows,
    tok_ref, rank_ref, prob_ref, prow_ref, pcol_ref, wg_hbm, wu_hbm, wd_hbm,
    out_ref,
    wg, wu, wd, part, over, sib, red, yrec, hid, eo, gmat,
    pout, pown, xrec, zout, zrec,
    gsem, usem, dsem, s1s, s1r, y1s, y1r, y2s, y2r, s2s, s2r, xs, xr, zs, zr,
):
    n_exp, db, ff = wg_hbm.shape
    tok_count = tok_ref.shape[0]
    slots, dslots = wg.shape[0], wd.shape[0]
    per = base // unit
    units = part.shape[0]
    pool_units = pool // unit
    spill = full_rows - base
    me = lax.axis_index("dp")
    core = lax.rem(me, CORES)
    row = me // CORES
    sibling = row * CORES + (1 - core)
    x, z = lax.axis_index("tensor"), lax.axis_index("expert")
    block = tok_count // (n_x * n_z)

    def y_peer(k):
        return lax.rem(row + k, n_y) * CORES + core

    def load_gu(e):
        at = lax.rem(e, slots)
        return (
            pltpu.make_async_copy(wg_hbm.at[e], wg.at[at], gsem.at[at]),
            pltpu.make_async_copy(wu_hbm.at[e], wu.at[at], usem.at[at]),
        )

    def load_d(e):
        at = lax.rem(e, dslots)
        return pltpu.make_async_copy(wd_hbm.at[e], wd.at[at], dsem.at[at])

    def send_half(u):
        return pltpu.make_async_remote_copy(
            part.at[u, 1 - core], sib.at[u], s1s.at[u], s1r.at[u], device_id={"dp": sibling})

    def send_term(u, k):
        return pltpu.make_async_remote_copy(
            red.at[u, lax.rem(row + k, n_y)], yrec.at[u, k - 1],
            y1s.at[u, k - 1], y1r.at[u, k - 1], device_id={"dp": y_peer(k)})

    def send_hidden(u, k):
        return pltpu.make_async_remote_copy(
            hid.at[u, core, row], hid.at[u, core, row],
            y2s.at[u, k - 1], y2r.at[u, k - 1], device_id={"dp": y_peer(k)})

    def send_group(u):
        return pltpu.make_async_remote_copy(
            hid.at[u, core], hid.at[u, core], s2s.at[u], s2r.at[u], device_id={"dp": sibling})

    def send_x(j, zz):
        there = lax.rem(x + j, n_x)
        return pltpu.make_async_remote_copy(
            pout.at[j - 1, zz], xrec.at[j - 1, zz], xs.at[j - 1, zz], xr.at[j - 1, zz],
            device_id={"tensor": there})

    def send_z(k):
        zz = lax.rem(z + k, n_z)
        return pltpu.make_async_remote_copy(
            zout.at[k - 1], zrec.at[k - 1], zs.at[k - 1], zr.at[k - 1], device_id={"expert": zz})

    for e in range(min(slots, n_exp)):
        for c in load_gu(e):
            c.start()
    for e in range(min(dslots, n_exp)):
        load_d(e).start()

    barrier = pltpu.get_barrier_semaphore()
    pl.semaphore_signal(barrier, inc=1, device_id={"dp": sibling})
    for k in range(1, n_y):
        pl.semaphore_signal(barrier, inc=1, device_id={"dp": y_peer(k)})
    for j in range(1, n_x):
        pl.semaphore_signal(barrier, inc=1, device_id={"tensor": lax.rem(x + j, n_x)})
    for k in range(1, n_z):
        pl.semaphore_signal(barrier, inc=1, device_id={"expert": lax.rem(z + k, n_z)})
    pl.semaphore_wait(barrier, n_y + n_x + n_z - 2)

    def onehot(e, at, size):
        rows = lax.broadcasted_iota(jnp.int32, (size, tok_count), 0) + at
        return rows == rank_ref[pl.ds(e, 1), :]

    def first(e):
        at = lax.rem(e, slots)
        for c in load_gu(e):
            c.wait()
        for r0, size in cut(full_rows, 128):
            x = jnp.dot(onehot(e, r0, size).astype(F32).astype(BF), tok_ref[...],
                        preferred_element_type=F32).astype(BF)
            for w, shift in ((wg, 0), (wu, ff)):
                for c0, width in cut(ff, 512):
                    p = jnp.dot(x, w[at, :, c0:c0 + width], preferred_element_type=F32).astype(BF)
                    cols = slice(shift + c0, shift + c0 + width)
                    step = min(size, unit // (CORES * n_y))
                    for r in range(0, size, step):
                        if r0 + r < base:
                            j = (r0 + r) // unit
                            left = (r0 + r) % unit
                            half = unit // CORES
                            part[e * per + j, left // half, (left % half) // step, :, cols] = p[r:r + step]
                    if spill and r0 + size > base:
                        lo = max(base - r0, 0)
                        over[pl.ds(pl.multiple_of(e * spill + r0 + lo - base, 16), size - lo), cols] = p[lo:]

        @pl.when(e + slots < n_exp)
        def _():
            for c in load_gu(e + slots):
                c.start()

        for j in range(per):
            send_half(e * per + j).start()

    def pooled():
        pick = (lax.broadcasted_iota(jnp.int32, (pool, n_exp * spill), 0) == prow_ref[...])
        pick = pick.astype(F32).astype(BF)
        for c0, width in cut(2 * ff, 512):
            p = jnp.dot(pick, over[:, c0:c0 + width], preferred_element_type=F32).astype(BF)
            part[n_exp * per:, :, :, :, c0:c0 + width] = p.reshape(
                (pool_units,) + part.shape[1:4] + (width,))
        for j in range(pool_units):
            send_half(n_exp * per + j).start()

    def second(u):
        send_half(u).wait_recv()
        for g in range(n_y):
            red[u, g] = (part[u, core, g].astype(F32) + sib[u, g].astype(F32)).astype(BF)
        for k in range(1, n_y):
            send_term(u, k).start()

    def third(u):
        for k in range(1, n_y):
            send_term(u, k).wait_recv()
        for c0, width in cut(ff, 512):
            g = red[u, row, :, c0:c0 + width].astype(F32)
            p = red[u, row, :, ff + c0:ff + c0 + width].astype(F32)
            for k in range(1, n_y):
                g += yrec[u, k - 1, :, c0:c0 + width].astype(F32)
                p += yrec[u, k - 1, :, ff + c0:ff + c0 + width].astype(F32)
            hid[u, core, row, :, c0:c0 + width] = (g / (1.0 + jnp.exp(-g)) * p).astype(BF)
        for k in range(1, n_y):
            send_hidden(u, k).start()

    def fourth(u):
        for k in range(1, n_y):
            send_hidden(u, k).wait_recv()
        send_group(u).start()

    lag_pair, lag_sum, lag_share = 1, 3, 5

    def on_units(step, do):
        @pl.when((step >= 0) & (step < n_exp))
        def _():
            for j in range(per):
                do(step * per + j)
        if pool:
            @pl.when((step >= n_exp) & (step < n_exp + pool_units))
            def _():
                do(n_exp * per + step - n_exp)

    def step(s, carry):
        @pl.when(s < n_exp)
        def _():
            first(s)
        if pool:
            @pl.when(s == n_exp)
            def _():
                pooled()
        on_units(s - lag_pair, second)
        on_units(s - lag_sum, third)
        on_units(s - lag_share, fourth)
        return carry

    lax.fori_loop(0, n_exp + pool_units + lag_share, step, 0)

    if pool:
        def arrived(j, carry):
            send_group(n_exp * per + j).wait_recv()
            return carry
        lax.fori_loop(0, pool_units, arrived, 0)

    def down(e, carry):
        at = lax.rem(e, dslots)
        for j in range(per):
            send_group(e * per + j).wait_recv()
        load_d(e).wait()
        rows = hid[pl.ds(e * per, per)].reshape(base, ff)
        if spill:
            mine = pcol_ref[pl.ds(pl.multiple_of(e * spill, 16), spill), :]
            pick = (lax.broadcasted_iota(jnp.int32, (spill, pool), 1) == mine).astype(F32).astype(BF)
            more = jnp.dot(pick, hid[n_exp * per:].reshape(pool, ff), preferred_element_type=F32)
            rows = jnp.concatenate([rows, more.astype(BF)], axis=0)
        for c0, width in cut(db, 512):
            y = jnp.dot(rows, wd[at, :, c0:c0 + width], preferred_element_type=F32).astype(BF)
            eo[pl.ds(pl.multiple_of(e * full_rows, 16), full_rows), c0:c0 + width] = y
        for r0, size in cut(full_rows, 128):
            gmat[pl.ds(pl.multiple_of(e * full_rows + r0, 16), size), :] = jnp.where(
                onehot(e, r0, size), prob_ref[pl.ds(e, 1), :], 0.0).astype(BF)

        @pl.when(e + dslots < n_exp)
        def _():
            load_d(e + dslots).start()
        return carry

    lax.fori_loop(0, n_exp, down, 0)
    span = n_z * block
    far = sorted(range(1, n_z), key=lambda k: -min(k, n_z - k))

    def combine(j, c0, width):
        at = pl.multiple_of(lax.rem(x + j, n_x) * span, span)
        y = lax.dot_general(
            gmat[:, pl.ds(at, span)], eo[:, c0:c0 + width], (((0,), (0,)), ((), ())),
            preferred_element_type=F32)
        return y.reshape(n_z, block, width)

    for j in range(1, n_x):
        for c0, width in cut(db, 512):
            pout[j - 1, :, :, c0:c0 + width] = combine(j, c0, width).astype(BF)
        for k in far + [0]:
            send_x(j, lax.rem(z + k, n_z)).start()
    for c0, width in cut(db, 512):
        pown[:, :, c0:c0 + width] = combine(0, c0, width)

    for k in far + [0]:
        zz = lax.rem(z + k, n_z)
        mine = pown[zz]
        for j in range(1, n_x):
            send_x(j, zz).wait_recv()
            mine += xrec[j - 1, zz].astype(F32)
        if k:
            zout[k - 1] = mine.astype(BF)
            send_z(k).start()
        else:
            pown[zz] = mine
    total = pown[z]
    for k in far[::-1]:
        send_z(k).wait_recv()
        total += zrec[k - 1].astype(F32)
    out_ref[...] = total.astype(BF)
    for k in far:
        send_z(k).wait_send()
    for j in range(1, n_x):
        for k in range(n_z):
            send_x(j, k).wait_send()

    def drain(u, carry):
        send_half(u).wait_send()
        for k in range(1, n_y):
            send_term(u, k).wait_send()
            send_hidden(u, k).wait_send()
        send_group(u).wait_send()
        return carry

    lax.fori_loop(0, units, drain, 0)


def run_experts(n_dp, n_x, n_z, base, pool, full_rows, ident, tok, rank, prob, wg, wu, wd):
    n_exp, db, ff = wg.shape
    n_y = n_dp // CORES
    unit = 16 * n_dp
    units = (n_exp * base + pool) // unit
    spill = full_rows - base
    tok_count = tok.shape[0]
    block = tok_count // (n_x * n_z)
    slots, dslots = min(3, n_exp), min(4, n_exp)
    if spill:
        extra = jnp.maximum(jnp.max(rank, axis=1) + 1 - base, 0)
        start = jnp.cumsum(extra) - extra
        place = (start[:, None] + jnp.arange(spill, dtype=jnp.int32)[None, :]).reshape(-1)
    else:
        place = jnp.zeros((16,), jnp.int32)
    group = (CORES, n_y, 16)
    vm = pltpu.VMEM
    dma = pltpu.SemaphoreType.DMA
    inside = pl.BlockSpec(memory_space=pltpu.VMEM)
    outside = pl.BlockSpec(memory_space=pl.ANY)
    return pl.pallas_call(
        functools.partial(experts_kernel, n_y, n_x, n_z, base, pool, unit, full_rows),
        out_shape=jax.ShapeDtypeStruct((block, db), BF),
        in_specs=[inside] * 5 + [outside] * 3,
        out_specs=inside,
        scratch_shapes=[
            vm((slots, db, ff), BF),
            vm((slots, db, ff), BF),
            vm((dslots, ff, db), BF),
            vm((units,) + group + (2 * ff,), BF),
            vm((n_exp * spill if spill else 16, 2 * ff), BF),
            vm((units, n_y, 16, 2 * ff), BF),
            vm((units, n_y, 16, 2 * ff), BF),
            vm((units, n_y - 1, 16, 2 * ff), BF),
            vm((units,) + group + (ff,), BF),
            vm((n_exp * full_rows, db), BF),
            vm((n_exp * full_rows, tok_count), BF),
            vm((n_x - 1, n_z, block, db), BF),
            vm((n_z, block, db), F32),
            vm((n_x - 1, n_z, block, db), BF),
            vm((n_z - 1, block, db), BF),
            vm((n_z - 1, block, db), BF),
            dma((slots,)), dma((slots,)), dma((dslots,)),
            dma((units,)), dma((units,)),
            dma((units, n_y - 1)), dma((units, n_y - 1)),
            dma((units, n_y - 1)), dma((units, n_y - 1)),
            dma((units,)), dma((units,)),
            dma((n_x - 1, n_z)), dma((n_x - 1, n_z)), dma((n_z - 1,)), dma((n_z - 1,)),
        ],
        compiler_params=pltpu.CompilerParams(
            collective_id=ident, has_side_effects=True, vmem_limit_bytes=61 * 1024 * 1024),
    )(tok, rank, prob, place.reshape(1, -1), place.reshape(-1, 1), wg, wu, wd)


def body(n_dp, tokens, routes, gate_probs, w_gate, w_up, w_down):
    group_tokens, top = routes.shape
    n_exp = w_gate.shape[0]
    n_x, n_z = lax.axis_size("tensor"), lax.axis_size("expert")
    owners = n_x * n_z
    mine = lax.axis_index("tensor") * n_z + lax.axis_index("expert")
    full_rows = owners * (2 * group_tokens * top // (owners * n_exp))
    info = jnp.concatenate([routes.astype(F32), gate_probs], axis=1).T
    tok, info = gather_all(n_x, n_z, tokens, info)
    tok = tok.reshape(owners * group_tokens, -1)
    info = info.transpose(0, 2, 1).reshape(owners * group_tokens, 2 * top)
    all_routes = info[:, :top].astype(jnp.int32)
    ids = mine * n_exp + jnp.arange(n_exp, dtype=jnp.int32)
    named = ids[:, None, None] == all_routes.T[None, :, :]
    chosen = jnp.any(named, axis=1)
    prob = jnp.sum(jnp.where(named, info[:, top:].T[None], 0.0), axis=1)
    count = all_routes.shape[0]
    before = lax.broadcasted_iota(jnp.int32, (count, count), 0) < lax.broadcasted_iota(
        jnp.int32, (count, count), 1)
    rank = jnp.dot(chosen.astype(BF), before.astype(BF), preferred_element_type=F32).astype(jnp.int32)
    rank = jnp.where(chosen, rank, -1)
    unit = 16 * n_dp
    args = (tok, rank, prob, w_gate, w_up, w_down)
    base, pool = full_rows // 2, n_exp * full_rows // 4
    if n_exp > 1 and base % unit == 0 and pool % unit == 0:
        everyone = jnp.arange(owners * n_exp, dtype=jnp.int32)
        loads = jnp.sum((all_routes.reshape(-1)[None, :] == everyone[:, None]).astype(jnp.int32), axis=1)
        extra = jnp.sum(jnp.maximum(loads - base, 0).reshape(owners, n_exp), axis=1)
        part = lax.cond(
            jnp.max(extra) <= pool,
            functools.partial(run_experts, n_dp, n_x, n_z, base, pool, full_rows, 1),
            functools.partial(run_experts, n_dp, n_x, n_z, full_rows, 0, full_rows, 2),
            *args)
    else:
        part = run_experts(n_dp, n_x, n_z, full_rows, 0, full_rows, 2, *args)
    return part


def solution(mesh):
    placed = (
        P(("tensor", "expert"), "dp"),
        P(("tensor", "expert"), None),
        P(("tensor", "expert"), None),
        P(("tensor", "expert"), "dp", None),
        P(("tensor", "expert"), "dp", None),
        P(("tensor", "expert"), None, "dp"),
    )
    return jax.shard_map(
        functools.partial(body, mesh.shape["dp"]), mesh=mesh, in_specs=placed,
        out_specs=P(("tensor", "expert"), "dp"), check_vma=False
    )
```

profile of v0, /device:TPU:0, one launch (start us, length us, event | category | flops | bytes accessed | tf_op | source)
XLA Modules:
  0.0 107.6 jit_solution(6643370441692755342)
XLA Ops:
  0.0 0.7 convert_element_type.17
  0.7 0.7 maximum_bitcast_fusion.info_ref
  1.4 0.0 copy-start
  1.4 0.9 copy-done
  2.3 23.3 %shard_map.66 = (bf16[8,64,1024]{2,1,0:T(8,128)(2,1)S(1)}, f32[8,16,64]{2,1,0:T(8,128)S(1)}) custom-call(bf16[64,1024]{1,0:T(8,128)(2,1)S(1)} %copy-done, f32[16,64]{1,0:T(8,128)S(1)} %maximum_bitcast_fusion.info_ref), custom_call_target="tpu_custom_call" | custom-call | tf_op jit(solution)/shard_map/pallas_call | solution.py:68
  25.7 0.1 reshape.100
  25.8 0.1 fusion.2
  25.9 0.1 compare_reduce_fusion
  26.0 0.2 fusion.1
  26.2 0.1 copy.16
  26.3 0.2 eq.28
  26.5 0.2 convert_reduce_fusion
  26.7 0.1 max.28
  26.8 0.1 reduce_sum.28
  26.9 0.6 reduce_max.18
  28.2 78.7 %conditional.1 = (bf16[64,1024]{1,0:T(8,128)(2,1)S(1)}) conditional(s32[]{:T(128)} %convert_element_type.20, (bf16[512,1024]{1,0:T(8,128)(2,1)S(1)}, s32[8,512]{1,0:T(8,128)S(1)}, f32[8,512]{1,0:T(8,128)S(1)}, bf16[8,1024,1536]{2,1,0:T(8,128)(2,1)}, bf16[8,1024,1536]{2,1,0:T(8,128)(2,1)}, /*index=5*/bf16[8,1536,1024]{2,1,0:T(8,128)(2,1)}) %tuple.19, ...), branch_computations={%region_5.6_spmd, %region_6.9_spmd} | conditional | flops 4696 | bytes 26928 | solution.py:420
  28.2 0.1 reduce_max.16
  28.3 0.2 reduce-window.7
  28.5 0.1 iota_add_fusion
  28.6 0.7 add.61.prow_ref
  29.3 0.9 add.69.pcol_ref
  30.1 76.8 %branch_1_fun.1 = bf16[64,1024]{1,0:T(8,128)(2,1)S(1)} custom-call(bf16[512,1024]{1,0:T(8,128)(2,1)S(1)} %get-tuple-element.38.tok_ref, s32[8,512]{1,0:T(8,128)S(1)} %get-tuple-element.39.rank_ref, f32[8,512]{1,0:T(8,128)S(1)} %get-tuple-element.40.prob_ref, s32[1,512]{1,0:T(1,128)} %add.61.prow_ref, s32[512,1]{1,0:T(8,128)} %add.69.pcol_ref, ...), custom_call_target="tpu_custom_call" | custom-call | tf_op jit(solution)/shard_map/cond/branch_1_fun/pallas_call | solution.py:358
  106.9 0.7 copy.20
  (6 shorter events, 0.1 us)
Async XLA Ops:
  1.4 0.9 copy-start
where the time goes:
time: 108 us
  Pallas kernels  100 us (93%)
  local copies, waits for them, and re-layouts  3.57 us (3%)
  other arithmetic  2.99 us (3%)
    pallas_call x1, Pallas kernels, run_experts(): pl.pallas_call(functools.partial(experts_kernel, n_y, n_x, n_z, base, poo...  76.8 us
    pallas_call x1, Pallas kernels, gather_all(): pl.pallas_call(functools.partial(gather_kernel, n_x, n_z), out_shape=[jax...  23.3 us

commit v1 on v0

--- a/solution.py
+++ b/solution.py
@@ -87,7 +87,7 @@
 ):
     n_exp, db, ff = wg_hbm.shape
     tok_count = tok_ref.shape[0]
-    slots, dslots = wg.shape[0], wd.shape[0]
+    slots = wg.shape[0]
     per = base // unit
     units = part.shape[0]
     pool_units = pool // unit
@@ -110,8 +110,7 @@
         )
 
     def load_d(e):
-        at = lax.rem(e, dslots)
-        return pltpu.make_async_copy(wd_hbm.at[e], wd.at[at], dsem.at[at])
+        return pltpu.make_async_copy(wd_hbm.at[e], wd.at[e], dsem.at[e])
 
     def send_half(u):
         return pltpu.make_async_remote_copy(
@@ -131,22 +130,20 @@
         return pltpu.make_async_remote_copy(
             hid.at[u, core], hid.at[u, core], s2s.at[u], s2r.at[u], device_id={"dp": sibling})
 
-    def send_x(j, zz):
+    def send_x(h, j, zz):
         there = lax.rem(x + j, n_x)
         return pltpu.make_async_remote_copy(
-            pout.at[j - 1, zz], xrec.at[j - 1, zz], xs.at[j - 1, zz], xr.at[j - 1, zz],
+            pout.at[h, j - 1, zz], xrec.at[h, j - 1, zz], xs.at[h, j - 1, zz], xr.at[h, j - 1, zz],
             device_id={"tensor": there})
 
-    def send_z(k):
+    def send_z(h, k):
         zz = lax.rem(z + k, n_z)
         return pltpu.make_async_remote_copy(
-            zout.at[k - 1], zrec.at[k - 1], zs.at[k - 1], zr.at[k - 1], device_id={"expert": zz})
+            zout.at[h, k - 1], zrec.at[h, k - 1], zs.at[h, k - 1], zr.at[h, k - 1], device_id={"expert": zz})
 
     for e in range(min(slots, n_exp)):
         for c in load_gu(e):
             c.start()
-    for e in range(min(dslots, n_exp)):
-        load_d(e).start()
 
     barrier = pltpu.get_barrier_semaphore()
     pl.semaphore_signal(barrier, inc=1, device_id={"dp": sibling})
@@ -189,6 +186,7 @@
             for c in load_gu(e + slots):
                 c.start()
 
+        load_d(e).start()
         for j in range(per):
             send_half(e * per + j).start()
 
@@ -260,69 +258,74 @@
             return carry
         lax.fori_loop(0, pool_units, arrived, 0)
 
-    def down(e, carry):
-        at = lax.rem(e, dslots)
+    def ready(e, carry):
         for j in range(per):
             send_group(e * per + j).wait_recv()
         load_d(e).wait()
-        rows = hid[pl.ds(e * per, per)].reshape(base, ff)
         if spill:
             mine = pcol_ref[pl.ds(pl.multiple_of(e * spill, 16), spill), :]
             pick = (lax.broadcasted_iota(jnp.int32, (spill, pool), 1) == mine).astype(F32).astype(BF)
             more = jnp.dot(pick, hid[n_exp * per:].reshape(pool, ff), preferred_element_type=F32)
-            rows = jnp.concatenate([rows, more.astype(BF)], axis=0)
-        for c0, width in cut(db, 512):
-            y = jnp.dot(rows, wd[at, :, c0:c0 + width], preferred_element_type=F32).astype(BF)
-            eo[pl.ds(pl.multiple_of(e * full_rows, 16), full_rows), c0:c0 + width] = y
+            over[pl.ds(pl.multiple_of(e * spill, 16), spill), :ff] = more.astype(BF)
         for r0, size in cut(full_rows, 128):
             gmat[pl.ds(pl.multiple_of(e * full_rows + r0, 16), size), :] = jnp.where(
                 onehot(e, r0, size), prob_ref[pl.ds(e, 1), :], 0.0).astype(BF)
-
-        @pl.when(e + dslots < n_exp)
-        def _():
-            load_d(e + dslots).start()
         return carry
 
-    lax.fori_loop(0, n_exp, down, 0)
-    span = n_z * block
+    lax.fori_loop(0, n_exp, ready, 0)
+
+    halves = cut(db, db // 2)
+    part_span = n_z * block
     far = sorted(range(1, n_z), key=lambda k: -min(k, n_z - k))
 
     def combine(j, c0, width):
-        at = pl.multiple_of(lax.rem(x + j, n_x) * span, span)
+        at = pl.multiple_of(lax.rem(x + j, n_x) * part_span, part_span)
         y = lax.dot_general(
-            gmat[:, pl.ds(at, span)], eo[:, c0:c0 + width], (((0,), (0,)), ((), ())),
+            gmat[:, pl.ds(at, part_span)], eo[:, c0:c0 + width], (((0,), (0,)), ((), ())),
             preferred_element_type=F32)
         return y.reshape(n_z, block, width)
 
-    for j in range(1, n_x):
-        for c0, width in cut(db, 512):
-            pout[j - 1, :, :, c0:c0 + width] = combine(j, c0, width).astype(BF)
+    for h, (c0, width) in enumerate(halves):
+        def down(e, carry, c0=c0, width=width):
+            rows = hid[pl.ds(e * per, per)].reshape(base, ff)
+            if spill:
+                more = over[pl.ds(pl.multiple_of(e * spill, 16), spill), :ff]
+                rows = jnp.concatenate([rows, more], axis=0)
+            y = jnp.dot(rows, wd[e, :, c0:c0 + width], preferred_element_type=F32).astype(BF)
+            eo[pl.ds(pl.multiple_of(e * full_rows, 16), full_rows), c0:c0 + width] = y
+            return carry
+
+        lax.fori_loop(0, n_exp, down, 0)
+        for j in range(1, n_x):
+            pout[h, j - 1] = combine(j, c0, width).astype(BF)
+            for k in far + [0]:
+                send_x(h, j, lax.rem(z + k, n_z)).start()
+        pown[h] = combine(0, c0, width)
+
+    for h in range(len(halves)):
         for k in far + [0]:
-            send_x(j, lax.rem(z + k, n_z)).start()
-    for c0, width in cut(db, 512):
-        pown[:, :, c0:c0 + width] = combine(0, c0, width)
-
-    for k in far + [0]:
-        zz = lax.rem(z + k, n_z)
-        mine = pown[zz]
+            zz = lax.rem(z + k, n_z)
+            mine = pown[h, zz]
+            for j in range(1, n_x):
+                send_x(h, j, zz).wait_recv()
+                mine += xrec[h, j - 1, zz].astype(F32)
+            if k:
+                zout[h, k - 1] = mine.astype(BF)
+                send_z(h, k).start()
+            else:
+                pown[h, zz] = mine
+    for h, (c0, width) in enumerate(halves):
+        total = pown[h, z]
+        for k in far[::-1]:
+            send_z(h, k).wait_recv()
+            total += zrec[h, k - 1].astype(F32)
+        out_ref[:, c0:c0 + width] = total.astype(BF)
+    for h in range(len(halves)):
+        for k in far:
+            send_z(h, k).wait_send()
         for j in range(1, n_x):
-            send_x(j, zz).wait_recv()
-            mine += xrec[j - 1, zz].astype(F32)
-        if k:
-            zout[k - 1] = mine.astype(BF)
-            send_z(k).start()
-        else:
-            pown[zz] = mine
-    total = pown[z]
-    for k in far[::-1]:
-        send_z(k).wait_recv()
-        total += zrec[k - 1].astype(F32)
-    out_ref[...] = total.astype(BF)
-    for k in far:
-        send_z(k).wait_send()
-    for j in range(1, n_x):
-        for k in range(n_z):
-            send_x(j, k).wait_send()
+            for k in range(n_z):
+                send_x(h, j, k).wait_send()
 
     def drain(u, carry):
         send_half(u).wait_send()
@@ -343,7 +346,7 @@
     spill = full_rows - base
     tok_count = tok.shape[0]
     block = tok_count // (n_x * n_z)
-    slots, dslots = min(3, n_exp), min(4, n_exp)
+    slots, dslots = min(2, n_exp), n_exp
     if spill:
         extra = jnp.maximum(jnp.max(rank, axis=1) + 1 - base, 0)
         start = jnp.cumsum(extra) - extra
@@ -372,17 +375,17 @@
             vm((units,) + group + (ff,), BF),
             vm((n_exp * full_rows, db), BF),
             vm((n_exp * full_rows, tok_count), BF),
-            vm((n_x - 1, n_z, block, db), BF),
-            vm((n_z, block, db), F32),
-            vm((n_x - 1, n_z, block, db), BF),
-            vm((n_z - 1, block, db), BF),
-            vm((n_z - 1, block, db), BF),
+            vm((2, n_x - 1, n_z, block, db // 2), BF),
+            vm((2, n_z, block, db // 2), F32),
+            vm((2, n_x - 1, n_z, block, db // 2), BF),
+            vm((2, n_z - 1, block, db // 2), BF),
+            vm((2, n_z - 1, block, db // 2), BF),
             dma((slots,)), dma((slots,)), dma((dslots,)),
             dma((units,)), dma((units,)),
             dma((units, n_y - 1)), dma((units, n_y - 1)),
             dma((units, n_y - 1)), dma((units, n_y - 1)),
             dma((units,)), dma((units,)),
-            dma((n_x - 1, n_z)), dma((n_x - 1, n_z)), dma((n_z - 1,)), dma((n_z - 1,)),
+            dma((2, n_x - 1, n_z)), dma((2, n_x - 1, n_z)), dma((2, n_z - 1)), dma((2, n_z - 1)),
         ],
         compiler_params=pltpu.CompilerParams(
             collective_id=ident, has_side_effects=True, vmem_limit_bytes=61 * 1024 * 1024),
@@ -412,15 +415,19 @@
     rank = jnp.where(chosen, rank, -1)
     unit = 16 * n_dp
     args = (tok, rank, prob, w_gate, w_up, w_down)
-    base, pool = full_rows // 2, n_exp * full_rows // 4
-    if n_exp > 1 and base % unit == 0 and pool % unit == 0:
+    base, quarter = full_rows // 2, n_exp * full_rows // 16
+    if n_exp > 1 and base % unit == 0 and quarter % unit == 0:
         everyone = jnp.arange(owners * n_exp, dtype=jnp.int32)
         loads = jnp.sum((all_routes.reshape(-1)[None, :] == everyone[:, None]).astype(jnp.int32), axis=1)
         extra = jnp.sum(jnp.maximum(loads - base, 0).reshape(owners, n_exp), axis=1)
-        part = lax.cond(
-            jnp.max(extra) <= pool,
-            functools.partial(run_experts, n_dp, n_x, n_z, base, pool, full_rows, 1),
-            functools.partial(run_experts, n_dp, n_x, n_z, full_rows, 0, full_rows, 2),
+        most = jnp.max(extra)
+        pools = (3 * quarter, 4 * quarter)
+        level = sum((most > p).astype(jnp.int32) for p in pools)
+        part = lax.switch(
+            level,
+            [functools.partial(run_experts, n_dp, n_x, n_z, base, p, full_rows, 4 + i)
+             for i, p in enumerate(pools)]
+            + [functools.partial(run_experts, n_dp, n_x, n_z, full_rows, 0, full_rows, 2)],
             *args)
     else:
         part = run_experts(n_dp, n_x, n_z, full_rows, 0, full_rows, 2, *args)

time: 108 us -> 104 us (0.963)
  Pallas kernels: 100 us -> 95.7 us
    pallas_call x1, Pallas kernels: 76.8 us -> 72.3 us  [run_experts(): pl.pallas_call(functools.partial(experts_kernel, n_y, n_x, n_z, base, poo...]
where the time goes in v1:
time: 104 us
  Pallas kernels  95.7 us (92%)
  local copies, waits for them, and re-layouts  3.57 us (3%)
  other arithmetic  2.99 us (3%)
  between operations  1.35 us (1%)
    pallas_call x1, Pallas kernels, run_experts(): pl.pallas_call(functools.partial(experts_kernel, n_y, n_x, n_z, base, poo...  72.3 us
    pallas_call x1, Pallas kernels, gather_all(): pl.pallas_call(functools.partial(gather_kernel, n_x, n_z), out_shape=[jax...  23.3 us

profile of v1, /device:TPU:0, one launch (start us, length us, event | category | flops | bytes accessed | tf_op | source)
XLA Modules:
  0.0 104.2 jit_solution(8059866715038165911)
XLA Ops:
  0.0 0.7 convert_element_type.20
  0.7 0.7 maximum_bitcast_fusion.info_ref
  1.4 0.0 copy-start
  1.4 0.9 copy-done
  2.3 23.3 %shard_map.67 = (bf16[8,64,1024]{2,1,0:T(8,128)(2,1)S(1)}, f32[8,16,64]{2,1,0:T(8,128)S(1)}) custom-call(bf16[64,1024]{1,0:T(8,128)(2,1)S(1)} %copy-done, f32[16,64]{1,0:T(8,128)S(1)} %maximum_bitcast_fusion.info_ref), custom_call_target="tpu_custom_call" | custom-call | tf_op jit(solution)/shard_map/pallas_call | solution.py:68
  25.7 0.1 reshape.181
  25.8 0.1 fusion.3
  25.9 0.1 compare_reduce_fusion
  26.0 0.2 fusion.2
  26.2 0.1 copy.19
  26.3 0.2 eq.28
  26.5 0.2 convert_reduce_fusion
  26.7 0.1 max.44
  26.8 0.1 reduce_sum.28
  26.9 0.6 reduce_max.27
  28.8 74.7 %conditional.1 = (bf16[64,1024]{1,0:T(8,128)(2,1)S(1)}) conditional(s32[]{:T(128)} %clamp.3, (s32[8,512]{1,0:T(8,128)S(1)}, bf16[512,1024]{1,0:T(8,128)(2,1)S(1)}, f32[8,512]{1,0:T(8,128)S(1)}, bf16[8,1024,1536]{2,1,0:T(8,128)(2,1)}, bf16[8,1024,1536]{2,1,0:T(8,128)(2,1)}, /*index=5*/bf16[8,1536,1024]{2,1,0:T(8,128)(2,1)}) %tuple.24, ...), branch_computations={%region_5.8_spmd, %region_8.11_spmd, %region_11.12_spmd} | conditional | flops 4696 | bytes 26928 | solution.py:426
  28.9 0.1 reduce_max.25
  29.0 0.2 reduce-window.15
  29.2 0.1 iota_add_fusion.1
  29.2 0.7 add.113.prow_ref
  29.9 0.9 add.124.pcol_ref
  30.8 72.3 %branch_1_fun.1 = bf16[64,1024]{1,0:T(8,128)(2,1)S(1)} custom-call(bf16[512,1024]{1,0:T(8,128)(2,1)S(1)} %get-tuple-element.51.tok_ref, s32[8,512]{1,0:T(8,128)S(1)} %get-tuple-element.52.rank_ref, f32[8,512]{1,0:T(8,128)S(1)} %get-tuple-element.53.prob_ref, s32[1,512]{1,0:T(1,128)} %add.113.prow_ref, s32[512,1]{1,0:T(8,128)} %add.124.pcol_ref, ...), custom_call_target="tpu_custom_call" | custom-call | tf_op jit(solution)/shard_map/cond/branch_1_fun/pallas_call | solution.py:361
  103.5 0.7 copy.24
  (6 shorter events, 0.1 us)
Async XLA Ops:
  1.4 0.9 copy-start
